TPU v7x, 256 devices: a whole 4x4x8 slice. The times are simulated.
256 devices in a mesh: dp: 32 (over x, z_lo, core), tensor: 8 (over z_hi, y).
Axes of the slice: x: 4, y: 4, z: 8 (z_hi: 2, z_lo: 4; z = z_hi * 4 + z_lo), core: 2. Of those that a mesh axis runs over, the one named last changes fastest.
Arguments:
- pool_rows: bfloat16 [8192, 28672], P('dp', 'tensor'), may hold values from -6 to 6
- out_grads: bfloat16 [131072, 8192], P('dp', 'tensor'), may hold values from -6 to 6
- proj_in: bfloat16 [28672, 64], P('tensor'), may hold values from -0.03125 to 0.03125
- proj_out: bfloat16 [8192, 64], P('tensor'), may hold values from -0.0625 to 0.0625
- token_ids: int32 [131072], P('dp'), may hold values from 0 to 255, as said below
- lengths: int32 [128], P('dp'), may hold values from 256 to 1024, as said below
- queries: bfloat16 [1024, 4096], P('dp', 'tensor'), may hold values from -0.099609375 to 0.099609375
Outputs:
- sketches: float32 [128, 4096], P('dp', 'tensor')
- scores: float32 [128, 1024], P('dp')
Inputs may be any that keep to these rules, and one draw needn't show every extreme that they name: `token_ids`: every dp block of 4096 slots uses row 0 and row 255 of its block. `lengths`: the first example of every dp block has all 1024 slots live.
All inputs are finite; a program needn't handle non-finite values.
Results may differ from a plain program's by a relative error of at most 0.0029.
Values may be sent and summed in bfloat16 or wider, within the bound.
A program may use at most 64 MiB of HBM per device.

v0:
```python
import jax
import jax.numpy as jnp
from jax import lax
from jax.sharding import PartitionSpec as P


def local(pool_rows, out_grads, proj_in, proj_out, token_ids, lengths, queries):
    width = proj_in.shape[1]
    groups = lax.axis_size("tensor")
    share = width // groups
    examples = lengths.shape[0]
    slots = out_grads.shape[0] // examples
    pool_part = jnp.dot(pool_rows, proj_in, preferred_element_type=jnp.float32)
    grad_part = jnp.dot(out_grads, proj_out, preferred_element_type=jnp.float32)
    place = jnp.arange(slots, dtype=jnp.int32)
    live = (place[None, :] < lengths[:, None]).astype(jnp.float32)
    weight = live * lax.rsqrt(lengths.astype(jnp.float32))[:, None]
    pool_proj, grad_full = lax.psum((pool_part, grad_part), "tensor")
    grad_mine = lax.dynamic_slice_in_dim(grad_full, lax.axis_index("tensor") * share, share, 1)
    in_proj = jnp.take(pool_proj, token_ids, axis=0)
    scaled = grad_mine.reshape(examples, slots, share) * weight[:, :, None]
    sketches = jnp.einsum(
        "tla,tlb->tab",
        scaled,
        in_proj.reshape(examples, slots, width),
        precision=lax.Precision.HIGHEST,
    ).reshape(examples, share * width)
    sketch_low = sketches.astype(jnp.bfloat16)
    partial_scores = jnp.einsum(
        "ek,qk->eq",
        sketch_low,
        lax.all_gather(queries, "dp", axis=0, tiled=True),
        preferred_element_type=jnp.float32,
    )
    scores = lax.psum(partial_scores, "tensor")
    return (sketches, scores)


def solution(mesh):
    return jax.shard_map(
        local,
        mesh=mesh,
        in_specs=(
            P("dp", "tensor"),
            P("dp", "tensor"),
            P("tensor", None),
            P("tensor", None),
            P("dp"),
            P("dp"),
            P("dp", "tensor"),
        ),
        out_specs=(P("dp", "tensor"), P("dp", None)),
        check_vma=False,
    )
```

profile of v0, /device:TPU:4, one launch (start us, length us, event | category | flops | bytes accessed | tf_op | source)
XLA Modules:
  0.0 212.2 jit_solution(17080186719263106395)
XLA Ops:
  8.0 0.0 copy-start
  8.0 0.0 copy-start.1
  8.0 0.0 all-reduce.3.cloned.1.call-start
  8.1 7.2 %fusion.11 = f32[4096,64]{0,1:T(8,128)} fusion(bf16[4096,1024]{1,0:T(8,128)(2,1)} %param.8, bf16[1024,64]{0,1:T(8,128)(2,1)} %param.10), kind=kOutput, calls=%fused_computation.17 | convolution fusion | flops 536870912 | bytes 9568256 | tf_op jit(solution)/shard_map/dot_general | solution.py:14
  15.2 0.0 copy-done
  15.2 0.0 copy-done.1
  15.2 0.0 copy-start.2
  15.2 0.0 copy-start.4
  15.2 1.3 fusion.12
  16.5 0.0 all-reduce.3.cloned.1.call-update
  16.6 0.0 all-gather.2.cloned.1.call-start
  16.6 0.5 all-gather.2.cloned.1.call-update
  17.1 0.0 copy-done.2
  17.2 0.0 copy-done.4
  17.2 0.1 fusion.6
  17.3 117.6 %all-reduce.3.cloned.1.call-done = (f32[256,64]{0,1:T(8,128)}, f32[4096,64]{0,1:T(8,128)}) async-done(((f32[256,64]{0,1:T(8,128)}, f32[4096,64]{0,1:T(8,128)}), (f32[256,64]{0,1:T(8,128)}, f32[4096,64]{0,1:T(8,128)})) %all-reduce.3.cloned.1.call-update) | async-done | bytes 1114128 | tf_op jit(solution)/shard_map/psum | solution.py:18
  134.9 0.9 copy.9
  135.8 14.1 %gather_fusion = f32[4096,64]{1,0:T(8,128)} fusion(f32[256,64]{1,0:T(8,128)S(1)} %copy.9, s32[4096]{0:T(1024)S(1)} %fusion.7), kind=kCustom, calls=%fused_computation | custom fusion | bytes 2113536 | tf_op jit(solution)/shard_map/jit(_take)/gather | solution.py:20
  149.9 2.2 %copy.10 = f32[4,1024,64]{1,2,0:T(8,128)S(1)} copy(f32[4,1024,64]{2,1,0:T(8,128)} %bitcast.7) | data formatting | bytes 2097152 | tf_op jit(solution)/shard_map/jit(_take)/gather | solution.py:20
  152.1 0.9 constant_dynamic-slice_fusion
  153.0 0.9 fusion
  153.9 0.1 reshape.60
  154.0 0.0 copy-start.3
  154.0 0.0 all-gather.2.cloned.1.call-done
  154.0 1.6 fusion.8
  155.6 49.1 %psum.23 = f32[4,1024]{1,0:T(4,128)} all-reduce(f32[4,1024]{1,0:T(4,128)S(1)} %fusion.8), channel_id=1, replica_groups=mesh['dp'=32,'tensor'=8] {'tensor'}, use_global_device_ids=true, to_apply=%region_2.3 | all-reduce | flops 4096 | bytes 32768 | tf_op jit(solution)/shard_map/psum | solution.py:35
  204.8 0.0 copy-done.3
  (4 shorter events, 0.0 us)
Async XLA Ops:
  8.0 7.2 %copy-start = (bf16[256,3584]{1,0:T(8,128)(2,1)S(1)}, bf16[256,3584]{1,0:T(8,128)(2,1)}, u32[]{:S(2)}) copy-start(bf16[256,3584]{1,0:T(8,128)(2,1)} %param.7) | copy-start | bytes 5505028
  8.0 7.2 %copy-start.1 = (bf16[3584,64]{0,1:T(8,128)(2,1)S(1)}, bf16[3584,64]{0,1:T(8,128)(2,1)}, u32[]{:S(2)}) copy-start(bf16[3584,64]{0,1:T(8,128)(2,1)} %param.9) | copy-start | bytes 1376260
  8.0 126.8 %all-reduce.3.cloned.1.call-start = ((), (), s32[]{:S(2)}) async-start(), calls=%async_computation.1 | async-start | bytes 2228224 | tf_op jit(solution)/shard_map/psum | solution.py:18
  15.2 1.9 copy-start.2
  15.2 2.0 copy-start.4
  16.6 137.5 %all-gather.2.cloned.1.call-start = ((), (), s32[]{:S(2)}) async-start(), calls=%async_computation | async-start | bytes 1081344 | tf_op jit(solution)/shard_map/all_gather | solution.py:32
  154.0 50.8 %copy-start.3 = (f32[4,512]{1,0:T(4,128)}, f32[4,512]{1,0:T(4,128)S(1)}, u32[]{:S(2)}) copy-start(f32[4,512]{1,0:T(4,128)S(1)} %reshape.60) | copy-start | bytes 24580
Sparse Core Ops, SparseCore 0:
  16.7 118.1 all-reduce.2
Sparse Core Ops, SparseCore 1:
  19.0 64.2 all-gather.1
where the time goes:
time: 212 us
  waiting for transfers between devices  118 us (56%)
  blocking collectives  49.1 us (23%)
  local copies, waits for them, and re-layouts  18.2 us (9%)
  between operations  15.6 us (7%)
  matrix products  11 us (5%)
    psum x1, waiting for transfers between devices, local(): pool_proj, grad_full = lax.psum((pool_part, grad_part), 'tensor')  118 us
    psum x1, blocking collectives, local(): scores = lax.psum(partial_scores, 'tensor')  49.1 us
    gather x2, local copies, waits for them, and re-layouts, local(): in_proj = jnp.take(pool_proj, token_ids, axis=0)  16.3 us
    dot_general x1, matrix products, local(): grad_part = jnp.dot(out_grads, proj_out, preferred_element_type=jnp.float32)  7.16 us
  transfers between devices with their start and end apart: 2, of which 1 were waited for; matrix products, arithmetic and copies ran while one was open for 9% of the time, Pallas kernels for 0%

commit v1 on v0

v1 whole, which is shorter than its diff:
```python
import jax
import jax.numpy as jnp
from jax import lax
from jax.experimental import pallas as pl
from jax.experimental.pallas import tpu as pltpu
from jax.sharding import PartitionSpec as P

F32, BF16 = jnp.float32, jnp.bfloat16
MESH = pl.DeviceIdType.MESH
T = 8
NX, NZ, NC = 4, 4, 2


def dot_nt(a, b):
    return lax.dot_general(a, b, (((1,), (1,)), ((), ())), preferred_element_type=F32)


def split(v):
    high = v.astype(BF16)
    return high, (v - high.astype(F32)).astype(BF16)


def kernel(
    pool, grads, pin, pout, ids, lens, qs,
    sk_out, sc_out,
    pool_v, grads_v, pin_v, pout_v, ids_v, lens_v, qall,
    p_send, p_recv, p_tot, s_send, s_recv, sk_v, c_send, c_recv, c_tot,
    in_sem, g_sem, q_local,
    qz_s, qz_r, qx_s, qx_r, qf_s, qf_r, qc_s, qc_r,
    p_s, p_r, a_s, a_r, s_s, s_r, c_s, c_r, d_s, d_r,
):
    me = lax.axis_index("tensor")
    dp = lax.axis_index("dp")
    x, z, c = dp // (NZ * NC), (dp // NC) % NZ, dp % NC
    examples, slots = grads_v.shape[:2]

    loads = [
        pltpu.make_async_copy(s, d, in_sem.at[i])
        for i, (s, d) in enumerate(
            [(pin, pin_v), (pool, pool_v), (pout, pout_v), (ids, ids_v), (lens, lens_v)]
        )
    ]
    for copy in loads:
        copy.start()
    chunks = [
        pltpu.make_async_copy(grads.at[pl.ds(e * slots, slots)], grads_v.at[e], g_sem.at[e])
        for e in range(examples)
    ]
    for copy in chunks:
        copy.start()
    own_q = pltpu.make_async_copy(qs, qall.at[x, z, c], q_local)
    own_q.start()

    def peer(k):
        return lax.rem(me + k, T)

    def source(k):
        return lax.rem(me + T - k, T)

    def device(px, pz, pc):
        return {"dp": (px * NZ + pz) * NC + pc}

    right, left, far = (x + 1) % NX, (x + 3) % NX, (x + 2) % NX
    z_peers = [(z + k) % NZ for k in range(1, NZ)]
    z_sources = [(z + NZ - k) % NZ for k in range(1, NZ)]

    barrier = pltpu.get_barrier_semaphore()
    friends = [{"tensor": peer(k)} for k in range(1, T)]
    friends += [device(x, pz, c) for pz in z_peers]
    friends += [device(right, z, c), device(left, z, c), device(x, z, 1 - c)]
    for friend in friends:
        pl.semaphore_signal(barrier, inc=1, device_id=friend, device_id_type=MESH)
    pl.semaphore_wait(barrier, len(friends))

    def remote(src, dst, send, recv, to):
        return pltpu.make_async_remote_copy(
            src_ref=src, dst_ref=dst, send_sem=send, recv_sem=recv,
            device_id=to, device_id_type=MESH,
        )

    q_z = [
        remote(qs, qall.at[x, z, c], qz_s.at[k], qz_r.at[k], device(x, z_peers[k], c))
        for k in range(NZ - 1)
    ]
    for copy in q_z:
        copy.start()

    loads[0].wait()
    loads[1].wait()
    p_send[...] = dot_nt(pin_v[...], pool_v[...]).reshape(p_send.shape)
    p_out = [
        remote(p_send.at[peer(k)], p_recv.at[me], p_s.at[k], p_r.at[k], {"tensor": peer(k)})
        for k in range(1, T)
    ]
    for copy in p_out:
        copy.start()
    p_recv[me] = p_send[me]

    for copy in loads[2:]:
        copy.wait()
    weights = pout_v[...]
    rows = lax.broadcasted_iota(jnp.int32, (pool_v.shape[0], 128), 0)
    lane = lax.broadcasted_iota(jnp.int32, (1, 128), 1)
    scale = lax.rsqrt(lens_v[...].astype(F32))
    half = 512

    def example(e):
        chunks[e].wait()
        length = lens_v[:, e:e + 1]
        total = None
        for h in range(slots // half):
            grad = dot_nt(weights, grads_v[e, h * half:(h + 1) * half, :])
            pick = []
            for j in range(half // 128):
                first = h * half + j * 128
                row = (e * slots + first) // 128
                token = jnp.where(lane + first < length, ids_v[row:row + 1, :], -1)
                pick.append(jnp.where(rows == token, 1.0, 0.0).astype(BF16))
            part = dot_nt(jnp.concatenate(split(grad), 0), jnp.concatenate(pick, 1))
            total = part if total is None else total + part
        low = total.shape[0] // 2
        total = (total[:low] + total[low:]) * scale[:, e:e + 1]
        s_send[e] = total.reshape(s_send.shape[1:])
        out = [
            remote(s_send.at[e, peer(k)], s_recv.at[e, me], s_s.at[e, k], s_r.at[e, k], {"tensor": peer(k)})
            for k in range(1, T)
        ]
        for copy in out:
            copy.start()
        s_recv[e, me] = s_send[e, me]
        return out

    s_out = [example(0)]

    own_q.wait()
    for copy in q_z:
        copy.wait_recv()
    mine = qall.at[x, :, c]
    q_x = [
        remote(mine, mine, qx_s.at[0], qx_r.at[0], device(right, z, c)),
        remote(mine, mine, qx_s.at[1], qx_r.at[1], device(left, z, c)),
    ]
    other = device(x, z, 1 - c)
    q_c = [remote(mine, mine, qc_s.at[0], qc_r.at[0], other)]
    for copy in q_x + q_c:
        copy.start()

    s_out.append(example(1))

    for copy in p_out:
        copy.wait_recv()
    p_tot[me] = jnp.sum(p_recv[...], axis=0)
    a_out = [
        remote(p_tot.at[me], p_tot.at[me], a_s.at[k], a_r.at[k], {"tensor": peer(k)})
        for k in range(1, T)
    ]
    for copy in a_out:
        copy.start()

    s_out.append(example(2))

    def waiter(dst, send, recv):
        return remote(dst, dst, send, recv, other)

    waiter(qall.at[left, :, c], qx_s.at[0], qx_r.at[0]).wait_recv()
    waiter(qall.at[right, :, c], qx_s.at[1], qx_r.at[1]).wait_recv()
    front, back = qall.at[left, 0:NZ // 2, c], qall.at[right, NZ // 2:NZ, c]
    q_f = [
        remote(front, front, qf_s.at[0], qf_r.at[0], device(right, z, c)),
        remote(back, back, qf_s.at[1], qf_r.at[1], device(left, z, c)),
    ]
    from_left, from_right = qall.at[left, :, c], qall.at[right, :, c]
    q_c += [
        remote(from_left, from_left, qc_s.at[1], qc_r.at[1], other),
        remote(from_right, from_right, qc_s.at[2], qc_r.at[2], other),
    ]
    for copy in q_f + q_c[1:]:
        copy.start()

    s_out.append(example(3))

    waiter(qall.at[far, 0:NZ // 2, c], qf_s.at[0], qf_r.at[0]).wait_recv()
    waiter(qall.at[far, NZ // 2:NZ, c], qf_s.at[1], qf_r.at[1]).wait_recv()
    from_far = qall.at[far, :, c]
    q_c.append(remote(from_far, from_far, qc_s.at[3], qc_r.at[3], other))
    q_c[3].start()

    for copy in a_out:
        copy.wait_recv()
    width = p_tot.shape[0] * p_tot.shape[1]
    p_high, p_low = split(p_tot[...].reshape(width, p_tot.shape[2]))

    totals = []
    for e in range(examples):
        for copy in s_out[e]:
            copy.wait_recv()
        totals.append(jnp.sum(s_recv[e], axis=0))
    t_high, t_low = split(jnp.concatenate(totals, 0))
    n = t_high.shape[0]
    both = dot_nt(jnp.concatenate([t_high, t_low], 0), p_high)
    sk_v[...] = both[:n] + both[n:] + dot_nt(t_high, p_low)
    share = s_recv.shape[2]
    flat = jnp.concatenate([sk_v[pl.ds(a, examples, stride=share), :] for a in range(share)], 1)
    sk_out[...] = flat

    waiter(qall.at[x, :, 1 - c], qc_s.at[0], qc_r.at[0]).wait_recv()
    waiter(qall.at[left, :, 1 - c], qc_s.at[1], qc_r.at[1]).wait_recv()
    waiter(qall.at[right, :, 1 - c], qc_s.at[2], qc_r.at[2]).wait_recv()
    waiter(qall.at[far, :, 1 - c], qc_s.at[3], qc_r.at[3]).wait_recv()
    queries = qall[...].reshape(T * 128, flat.shape[1])
    part = dot_nt(flat.astype(BF16), queries)
    for t in range(T):
        c_send[t] = part[:, t * 128:(t + 1) * 128]
    c_out = [
        remote(c_send.at[peer(k)], c_recv.at[me], c_s.at[k], c_r.at[k], {"tensor": peer(k)})
        for k in range(1, T)
    ]
    for copy in c_out:
        copy.start()
    c_recv[me] = c_send[me]
    for copy in c_out:
        copy.wait_recv()
    c_tot[me] = jnp.sum(c_recv[...], axis=0)
    d_out = [
        remote(c_tot.at[me], c_tot.at[me], d_s.at[k], d_r.at[k], {"tensor": peer(k)})
        for k in range(1, T)
    ]
    for copy in d_out:
        copy.start()
    for copy in d_out:
        copy.wait_recv()
    for t in range(T):
        sc_out[:, t * 128:(t + 1) * 128] = c_tot[t]

    for copy in q_z + q_x + q_f + q_c + p_out + a_out + sum(s_out, []) + c_out + d_out:
        copy.wait_send()


def local(pool_rows, out_grads, proj_in, proj_out, token_ids, lengths, queries):
    examples = lengths.shape[0]
    slots = out_grads.shape[0] // examples
    width = proj_in.shape[1]
    share = width // T
    pool = pool_rows.shape[0]
    model = out_grads.shape[1]
    rows, cols = queries.shape
    any_spec = pl.BlockSpec(memory_space=pltpu.HBM)
    dma = pltpu.SemaphoreType.DMA
    vmem = pltpu.VMEM
    return pl.pallas_call(
        kernel,
        out_shape=(
            jax.ShapeDtypeStruct((examples, share * width), F32),
            jax.ShapeDtypeStruct((examples, rows * NX * NZ * NC), F32),
        ),
        in_specs=[any_spec] * 7,
        out_specs=[pl.BlockSpec(memory_space=pltpu.VMEM)] * 2,
        scratch_shapes=[
            vmem(pool_rows.shape, BF16),
            vmem((examples, slots, model), BF16),
            vmem(proj_in.shape[::-1], BF16),
            vmem(proj_out.shape[::-1], BF16),
            vmem((token_ids.shape[0] // 128, 128), jnp.int32),
            vmem((1, examples), jnp.int32),
            vmem((NX, NZ, NC, rows, cols), BF16),
            vmem((T, share, pool), F32),
            vmem((T, share, pool), F32),
            vmem((T, share, pool), F32),
            vmem((examples, T, share, pool), F32),
            vmem((examples, T, share, pool), F32),
            vmem((examples * share, width), F32),
            vmem((T, examples, 128), F32),
            vmem((T, examples, 128), F32),
            vmem((T, examples, 128), F32),
            dma((5,)), dma((examples,)), dma(()),
            dma((3,)), dma((3,)), dma((2,)), dma((2,)), dma((2,)), dma((2,)), dma((4,)), dma((4,)),
            dma((T,)), dma((T,)), dma((T,)), dma((T,)),
            dma((examples, T)), dma((examples, T)),
            dma((T,)), dma((T,)), dma((T,)), dma((T,)),
        ],
        compiler_params=pltpu.CompilerParams(
            collective_id=0, has_side_effects=True, vmem_limit_bytes=48 * 1024 * 1024
        ),
    )(
        pool_rows, out_grads, proj_in.T, proj_out.T,
        token_ids.reshape(-1, 128), lengths.reshape(1, -1), queries,
    )


def solution(mesh):
    return jax.shard_map(
        local,
        mesh=mesh,
        in_specs=(
            P("dp", "tensor"),
            P("dp", "tensor"),
            P("tensor", None),
            P("tensor", None),
            P("dp"),
            P("dp"),
            P("dp", "tensor"),
        ),
        out_specs=(P("dp", "tensor"), P("dp", None)),
        check_vma=False,
    )
```

time: 212 us -> 49.5 us (0.23)
  waiting for transfers between devices: 118 us -> 0 us
  blocking collectives: 49.1 us -> 0 us
  Pallas kernels: 0 us -> 41.7 us
  between operations: 15.6 us -> 0.65 us
  local copies, waits for them, and re-layouts: 18.2 us -> 6.75 us
  matrix products: 11 us -> 0 us
    psum x1 -> x0, waiting for transfers between devices: 118 us -> none  [local(): pool_proj, grad_full = lax.psum((pool_part, grad_part), 'tensor')]
    psum x1 -> x0, blocking collectives: 49.1 us -> none  [local(): scores = lax.psum(partial_scores, 'tensor')]
    pallas_call x0 -> x1, Pallas kernels: none -> 41.7 us  [local(): pl.pallas_call(kernel, out_shape=(jax.ShapeDtypeStruct((examples, share *...]
    gather x2 -> x0, local copies, waits for them, and re-layouts: 16.3 us -> none  [local(): in_proj = jnp.take(pool_proj, token_ids, axis=0)]
    dot_general x4 -> x0, matrix products: 11 us -> none  [the longest x1 7.16 us: local(): grad_part = jnp.dot(out_grads, proj_out, preferred_element_type=jnp.float32)]
    unnamed x10 -> x14, local copies, waits for them, and re-layouts: 0.03 us -> 6.75 us
  transfers between devices with their start and end apart: 2 -> 0, of which waited for: 1 -> 0; matrix products, arithmetic and copies ran while one was open for 9% -> 0% of each run, Pallas kernels for 0% -> 0%
where the time goes in v1:
time: 49.5 us; the launch traced here: 49.2 us
  Pallas kernels  41.7 us (84%)
  local copies, waits for them, and re-layouts  6.75 us (14%)
  between operations  0.65 us (1%)
    pallas_call x1, Pallas kernels, local(): pl.pallas_call(kernel, out_shape=(jax.ShapeDtypeStruct((examples, share *...  41.7 us
    unnamed x14, local copies, waits for them, and re-layouts  6.75 us

profile of v1, /device:TPU:4, one launch (start us, length us, event | category | flops | bytes accessed | tf_op | source)
XLA Modules:
  0.0 49.2 jit_solution(10872978371669698765)
XLA Ops:
  0.6 0.0 copy-start
  0.6 1.5 %copy-done = bf16[256,3584]{1,0:T(8,128)(2,1)S(1)} copy-done((bf16[256,3584]{1,0:T(8,128)(2,1)S(1)}, bf16[256,3584]{1,0:T(8,128)(2,1)}, u32[]{:S(2)}) %copy-start) | copy-done | bytes 1835032
  2.1 0.0 copy-start.1
  2.1 1.0 %copy-done.1 = bf16[3584,64]{0,1:T(8,128)(2,1)S(1)} copy-done((bf16[3584,64]{0,1:T(8,128)(2,1)S(1)}, bf16[3584,64]{0,1:T(8,128)(2,1)}, u32[]{:S(2)}) %copy-start.1) | copy-done | bytes 458776
  3.2 0.0 copy-start.2
  3.2 0.9 %copy-done.2 = bf16[1024,64]{0,1:T(8,128)(2,1)S(1)} copy-done((bf16[1024,64]{0,1:T(8,128)(2,1)S(1)}, bf16[1024,64]{0,1:T(8,128)(2,1)}, u32[]{:S(2)}) %copy-start.2) | copy-done | bytes 131096
  4.1 0.0 copy-start.3
  4.1 0.8 %copy-done.3 = bf16[32,512]{1,0:T(8,128)(2,1)S(1)} copy-done((bf16[32,512]{1,0:T(8,128)(2,1)S(1)}, bf16[32,512]{1,0:T(8,128)(2,1)}, u32[]{:S(2)}) %copy-start.3) | copy-done | bytes 32792
  4.8 0.0 copy-start.4
  4.8 0.7 %copy-done.4 = s32[4096]{0:T(1024)S(1)} copy-done((s32[4096]{0:T(1024)S(1)}, s32[4096]{0:T(1024)}, u32[]{:S(2)}) %copy-start.4) | copy-done | bytes 16408
  5.5 0.0 copy-start.5
  5.5 0.7 %copy-done.5 = s32[4]{0:T(128)S(1)} copy-done((s32[4]{0:T(128)S(1)}, s32[4]{0:T(128)}, u32[]{:S(2)}) %copy-start.5) | copy-done | bytes 40
  6.2 41.7 %shard_map.86 = (f32[4,512]{1,0:T(4,128)S(1)}, f32[4,1024]{1,0:T(4,128)S(1)}) custom-call(bf16[256,3584]{1,0:T(8,128)(2,1)S(1)} %copy-done, bf16[4096,1024]{1,0:T(8,128)(2,1)} %grads.1, bf16[64,3584]{1,0:T(8,128)(2,1)S(1)} %bitcast.4, bf16[64,1024]{1,0:T(8,128)(2,1)S(1)} %bitcast.5, s32[32,128]{1,0:T(8,128)S(1)} %bitcast.6, s32[1,4]{1,0:T(1,128)S(1)} %bitcast.7, ...), custom_call_target="tpu_custom_call" | custom-call | tf_op jit(solution)/shard_map/pallas_call | solution.py:250
  47.9 0.6 %copy.11 = f32[4,512]{1,0:T(4,128)} copy(f32[4,512]{1,0:T(4,128)S(1)} %get-tuple-element.4) | data formatting | bytes 16384
  48.5 0.6 %copy.12 = f32[4,1024]{1,0:T(4,128)} copy(f32[4,1024]{1,0:T(4,128)S(1)} %get-tuple-element.5) | data formatting | bytes 32768
Async XLA Ops:
  0.6 1.5 %copy-start = (bf16[256,3584]{1,0:T(8,128)(2,1)S(1)}, bf16[256,3584]{1,0:T(8,128)(2,1)}, u32[]{:S(2)}) copy-start(bf16[256,3584]{1,0:T(8,128)(2,1)} %pool.1) | copy-start | bytes 5505028
  2.1 1.0 %copy-start.1 = (bf16[3584,64]{0,1:T(8,128)(2,1)S(1)}, bf16[3584,64]{0,1:T(8,128)(2,1)}, u32[]{:S(2)}) copy-start(bf16[3584,64]{0,1:T(8,128)(2,1)} %param.9) | copy-start | bytes 1376260
  3.2 0.9 %copy-start.2 = (bf16[1024,64]{0,1:T(8,128)(2,1)S(1)}, bf16[1024,64]{0,1:T(8,128)(2,1)}, u32[]{:S(2)}) copy-start(bf16[1024,64]{0,1:T(8,128)(2,1)} %param.10) | copy-start | bytes 393220
  4.1 0.8 %copy-start.3 = (bf16[32,512]{1,0:T(8,128)(2,1)S(1)}, bf16[32,512]{1,0:T(8,128)(2,1)}, u32[]{:S(2)}) copy-start(bf16[32,512]{1,0:T(8,128)(2,1)} %qs.1) | copy-start | bytes 98308
  4.8 0.7 %copy-start.4 = (s32[4096]{0:T(1024)S(1)}, s32[4096]{0:T(1024)}, u32[]{:S(2)}) copy-start(s32[4096]{0:T(1024)} %param.11) | copy-start | bytes 49156
  5.5 0.7 %copy-start.5 = (s32[4]{0:T(128)S(1)}, s32[4]{0:T(128)}, u32[]{:S(2)}) copy-start(s32[4]{0:T(128)} %param.12) | copy-start | bytes 52

commit v2 on v0

v2 whole, which is shorter than its diff:
```python
import jax
import jax.numpy as jnp
from jax import lax
from jax.experimental import pallas as pl
from jax.experimental.pallas import tpu as pltpu
from jax.sharding import PartitionSpec as P

F32, BF16 = jnp.float32, jnp.bfloat16
MESH = pl.DeviceIdType.MESH
T = 8
NY = 4
NX, NZ, NC = 4, 4, 2


def dot_nt(a, b):
    return lax.dot_general(a, b, (((1,), (1,)), ((), ())), preferred_element_type=F32)


def split(v):
    high = v.astype(BF16)
    return high, (v - high.astype(F32)).astype(BF16)


def kernel(
    pool, grads, pin, pout, ids, lens, qs,
    sk_out, sc_out,
    pool_v, grads_v, pin_v, pout_v, ids_v, lens_v, qall, pick_v, cat_v,
    p_send, p_recv, p_part, s_send, s_recv, z_send, z_recv, sk_v, c_send, c_recv,
    in_sem, g_sem, q_local,
    qz_s, qz_r, qx_s, qx_r, qc_s, qc_r,
    p_s, p_r, a_s, a_r, s_s, s_r, z_s, z_r, c_s, c_r,
):
    me = lax.axis_index("tensor")
    dp = lax.axis_index("dp")
    zh, y = me // NY, me % NY
    x, z, c = dp // (NZ * NC), (dp // NC) % NZ, dp % NC
    examples, slots = grads_v.shape[:2]

    loads = [
        pltpu.make_async_copy(s, d, in_sem.at[i])
        for i, (s, d) in enumerate(
            [(ids, ids_v), (lens, lens_v), (pin, pin_v), (pool, pool_v), (pout, pout_v)]
        )
    ]
    for copy in loads:
        copy.start()
    chunks = [
        pltpu.make_async_copy(grads.at[pl.ds(e * slots, slots)], grads_v.at[e], g_sem.at[e])
        for e in range(examples)
    ]
    for copy in chunks:
        copy.start()
    own_q = pltpu.make_async_copy(qs, qall.at[x, z, c], q_local)
    own_q.start()

    def device(px, pz, pc):
        return {"dp": (px * NZ + pz) * NC + pc}

    def peer(k):
        return lax.rem(me + k, T)

    y_to = [(y + k) % NY for k in range(1, NY)]
    z_to = [(z + k) % NZ for k in range(1, NZ)]
    z_from = [(z + NZ - k) % NZ for k in range(1, NZ)]
    x_to = [(x + k) % NX for k in range(1, NX)]
    x_from = [(x + NX - k) % NX for k in range(1, NX)]
    other = device(x, z, 1 - c)
    partner = {"tensor": (1 - zh) * NY + y}

    barrier = pltpu.get_barrier_semaphore()
    friends = [partner, other]
    friends += [{"tensor": zh * NY + p} for p in y_to]
    friends += [device(x, p, c) for p in z_to]
    friends += [device(p, z, c) for p in x_to]
    for friend in friends:
        pl.semaphore_signal(barrier, inc=1, device_id=friend, device_id_type=MESH)

    def remote(src, dst, send, recv, to):
        return pltpu.make_async_remote_copy(
            src_ref=src, dst_ref=dst, send_sem=send, recv_sem=recv,
            device_id=to, device_id_type=MESH,
        )

    def start(copies):
        for copy in copies:
            copy.start()
        sent.extend(copies)

    sent = []

    for copy in loads[:4]:
        copy.wait()
    p_send[...] = dot_nt(pin_v[...], pool_v[...]).reshape(p_send.shape)
    rows = lax.broadcasted_iota(jnp.int32, (pool_v.shape[0], 128), 0)
    lane = lax.broadcasted_iota(jnp.int32, (1, 128), 1)
    scale = lax.rsqrt(lens_v[...].astype(F32))
    for e in range(examples):
        length = lens_v[:, e:e + 1]
        for first in range(0, slots, 128):
            row = (e * slots + first) // 128
            token = jnp.where(lane + first < length, ids_v[row:row + 1, :], -1)
            pick_v[e, :, first:first + 128] = jnp.where(rows == token, 1.0, 0.0).astype(BF16)
    loads[4].wait()

    def project(e):
        chunks[e].wait()
        high, low = split(dot_nt(pout_v[...], grads_v[e]))
        n = high.shape[0]
        cat_v[e % 2, :n, :] = high
        cat_v[e % 2, n:, :] = low

    def gather(e):
        both = dot_nt(cat_v[e % 2], pick_v[e])
        n = both.shape[0] // 2
        total = ((both[:n] + both[n:]) * scale[:, e:e + 1]).astype(BF16)
        share = n // T
        for p in range(NY):
            s_send[p, e, :share] = total[p * share:(p + 1) * share]
            s_send[p, e, share:] = total[n // 2 + p * share:n // 2 + (p + 1) * share]

    project(0)
    project(1)
    gather(0)

    pl.semaphore_wait(barrier, len(friends))
    p_out = [
        remote(p_send.at[p], p_recv.at[y], p_s.at[k], p_r.at[k], {"tensor": zh * NY + p})
        for k, p in enumerate(y_to)
    ]
    start(p_out)
    q_z = [
        remote(qs, qall.at[x, z, c], qz_s.at[k], qz_r.at[k], device(x, p, c))
        for k, p in enumerate(z_to)
    ]
    start(q_z)

    def along_x(step, pz):
        block = qall.at[x, pz, c]
        return [
            remote(block, block, qx_s.at[k, step], qx_r.at[k, step], device(p, z, c))
            for k, p in enumerate(x_to)
        ]

    own_q.wait()
    start(along_x(0, z))

    project(2)
    gather(1)
    project(3)
    gather(2)
    gather(3)
    s_out = [
        remote(s_send.at[p], s_recv.at[y], s_s.at[k], s_r.at[k], {"tensor": zh * NY + p})
        for k, p in enumerate(y_to)
    ]
    start(s_out)

    p_recv[y] = p_send[y]
    for copy in p_out:
        copy.wait_recv()
    p_part[me] = jnp.sum(p_recv[...], axis=0)
    a_out = [
        remote(p_part.at[me], p_part.at[me], a_s.at[k - 1], a_r.at[k - 1], {"tensor": peer(k)})
        for k in range(1, T)
    ]
    start(a_out)

    for k in range(NZ - 1):
        remote(qs, qall.at[x, z_from[k], c], qz_s.at[k], qz_r.at[k], other).wait_recv()
        start(along_x(k + 1, z_from[k]))

    def across(k, px):
        line = qall.at[px, :, c]
        return remote(line, line, qc_s.at[k], qc_r.at[k], other)

    start([across(0, x)])

    s_recv[y] = s_send[y]
    for copy in s_out:
        copy.wait_recv()
    over_y = s_recv[0].astype(F32)
    for p in range(1, NY):
        over_y = over_y + s_recv[p].astype(F32)
    z_send[...] = over_y.reshape(z_send.shape)
    z_out = remote(z_send.at[:, 1 - zh], z_recv, z_s, z_r, partner)
    start([z_out])

    for k in range(NX - 1):
        for step in range(NZ):
            pz = z if step == 0 else z_from[step - 1]
            block = qall.at[x_from[k], pz, c]
            remote(block, block, qx_s.at[k, step], qx_r.at[k, step], other).wait_recv()
        start([across(k + 1, x_from[k])])

    for copy in a_out:
        copy.wait_recv()
    p_all = p_part[0:NY] + p_part[NY:T]
    p_high, p_low = split(p_all.reshape(NY * p_all.shape[1], p_all.shape[2]))

    z_out.wait_recv()
    mine = z_send[:, zh] + z_recv[...]
    share = mine.shape[1]
    t_high, t_low = split(mine.reshape(examples * share, mine.shape[2]))
    n = t_high.shape[0]
    both = dot_nt(jnp.concatenate([t_high, t_low], 0), p_high)
    sk_v[...] = both[:n] + both[n:] + dot_nt(t_high, p_low)
    flat = jnp.concatenate([sk_v[pl.ds(a, examples, stride=share), :] for a in range(share)], 1)
    sk_out[...] = flat

    for k in range(NX):
        px = x if k == 0 else x_from[k - 1]
        line = qall.at[px, :, 1 - c]
        remote(line, line, qc_s.at[k], qc_r.at[k], other).wait_recv()
    queries = qall[...].reshape(-1, flat.shape[1])
    part = dot_nt(jnp.concatenate(split(flat), 0), queries)
    c_send[...] = part[:examples] + part[examples:]
    c_out = [
        remote(c_send, c_recv.at[me], c_s.at[k - 1], c_r.at[k - 1], {"tensor": peer(k)})
        for k in range(1, T)
    ]
    start(c_out)
    c_recv[me] = c_send[...]
    for copy in c_out:
        copy.wait_recv()
    sc_out[...] = jnp.sum(c_recv[...], axis=0)

    for copy in sent:
        copy.wait_send()


def finish(a, b, a_out, b_out, sems):
    copies = [pltpu.make_async_copy(a, a_out, sems.at[0]), pltpu.make_async_copy(b, b_out, sems.at[1])]
    for copy in copies:
        copy.start()
    for copy in copies:
        copy.wait()


def local(pool_rows, out_grads, proj_in, proj_out, token_ids, lengths, queries):
    examples = lengths.shape[0]
    slots = out_grads.shape[0] // examples
    width = proj_in.shape[1]
    share = width // T
    pool = pool_rows.shape[0]
    model = out_grads.shape[1]
    rows, cols = queries.shape
    any_spec = pl.BlockSpec(memory_space=pl.ANY)
    dma = pltpu.SemaphoreType.DMA
    vmem = pltpu.VMEM
    sketches, scores = pl.pallas_call(
        kernel,
        out_shape=(
            jax.ShapeDtypeStruct((examples, share * width), F32),
            jax.ShapeDtypeStruct((examples, rows * NX * NZ * NC), F32),
        ),
        in_specs=[any_spec] * 7,
        out_specs=[pl.BlockSpec(memory_space=pltpu.VMEM)] * 2,
        scratch_shapes=[
            vmem(pool_rows.shape, BF16),
            vmem((examples, slots, model), BF16),
            vmem(proj_in.shape[::-1], BF16),
            vmem(proj_out.shape[::-1], BF16),
            vmem((token_ids.shape[0] // 128, 128), jnp.int32),
            vmem((1, examples), jnp.int32),
            vmem((NX, NZ, NC, rows, cols), BF16),
            vmem((examples, pool, slots), BF16),
            vmem((2, 2 * width, slots), BF16),
            vmem((NY, width // NY, pool), F32),
            vmem((NY, width // NY, pool), F32),
            vmem((T, width // NY, pool), F32),
            vmem((NY, examples, 2 * share, pool), BF16),
            vmem((NY, examples, 2 * share, pool), BF16),
            vmem((examples, 2, share, pool), F32),
            vmem((examples, share, pool), F32),
            vmem((examples * share, width), F32),
            vmem((examples, rows * NX * NZ * NC), F32),
            vmem((T, examples, rows * NX * NZ * NC), F32),
            dma((5,)), dma((examples,)), dma(()),
            dma((3,)), dma((3,)), dma((3, NZ)), dma((3, NZ)), dma((NX,)), dma((NX,)),
            dma((3,)), dma((3,)), dma((T - 1,)), dma((T - 1,)),
            dma((3,)), dma((3,)), dma(()), dma(()), dma((T - 1,)), dma((T - 1,)),
        ],
        compiler_params=pltpu.CompilerParams(
            collective_id=0, has_side_effects=True, vmem_limit_bytes=60 * 1024 * 1024
        ),
    )(
        pool_rows, out_grads, proj_in.T, proj_out.T,
        token_ids.reshape(-1, 128), lengths.reshape(1, -1), queries,
    )
    return pl.pallas_call(
        finish,
        out_shape=(
            jax.ShapeDtypeStruct(sketches.shape, F32),
            jax.ShapeDtypeStruct(scores.shape, F32),
        ),
        in_specs=[any_spec] * 2,
        out_specs=[any_spec] * 2,
        scratch_shapes=[dma((2,))],
        compiler_params=pltpu.CompilerParams(vmem_limit_bytes=60 * 1024 * 1024),
    )(sketches, scores)


def solution(mesh):
    return jax.shard_map(
        local,
        mesh=mesh,
        in_specs=(
            P("dp", "tensor"),
            P("dp", "tensor"),
            P("tensor", None),
            P("tensor", None),
            P("dp"),
            P("dp"),
            P("dp", "tensor"),
        ),
        out_specs=(P("dp", "tensor"), P("dp", None)),
        check_vma=False,
    )
```

time: 212 us -> 38.6 us (0.18)
  the two profiles are of different devices: /device:TPU:4 before, /device:TPU:1 now
where the time goes in v2:
time: 38.6 us; the launch traced here: 38.5 us
  Pallas kernels  37.8 us (98%)
  between operations  0.64 us (2%)
    pallas_call x1, Pallas kernels, local(): pl.pallas_call(kernel, out_shape=(jax.ShapeDtypeStruct((examples, share *...  36 us
    pallas_call x1, Pallas kernels, local(): pl.pallas_call(finish, out_shape=(jax.ShapeDtypeStruct(sketches.shape, F3...  1.87 us

profile of v2, /device:TPU:1, one launch (start us, length us, event | category | flops | bytes accessed | tf_op | source)
XLA Modules:
  0.0 38.5 jit_solution(2490809539608029570)
XLA Ops:
  0.6 36.0 %shard_map.86 = (f32[4,512]{1,0:T(4,128)}, f32[4,1024]{1,0:T(4,128)}) custom-call(bf16[256,3584]{1,0:T(8,128)(2,1)} %pool.1, bf16[4096,1024]{1,0:T(8,128)(2,1)} %grads.1, bf16[64,3584]{1,0:T(8,128)(2,1)} %bitcast.4, bf16[64,1024]{1,0:T(8,128)(2,1)} %bitcast.5, s32[32,128]{1,0:T(8,128)} %bitcast.6, s32[1,4]{1,0:T(1,128)} %bitcast.7, bf16[32,512]{1,0:T(8,128)(2,1)} %qs.1), custom_call_target="tpu_custom_call" | custom-call | tf_op jit(solution)/shard_map/pallas_call | solution.py:250
  36.6 1.9 %shard_map.87 = (f32[4,512]{1,0:T(4,128)}, f32[4,1024]{1,0:T(4,128)}) custom-call(f32[4,512]{1,0:T(4,128)} %get-tuple-element.4.a, f32[4,1024]{1,0:T(4,128)} %get-tuple-element.5.b), custom_call_target="tpu_custom_call" | custom-call | tf_op jit(solution)/shard_map/pallas_call | solution.py:290

commit v3 on v2

--- a/solution.py
+++ b/solution.py
@@ -9,6 +9,7 @@
 MESH = pl.DeviceIdType.MESH
 T = 8
 NY = 4
+GATES = 3, 0
 NX, NZ, NC = 4, 4, 2
 
 
@@ -36,23 +37,6 @@
     x, z, c = dp // (NZ * NC), (dp // NC) % NZ, dp % NC
     examples, slots = grads_v.shape[:2]
 
-    loads = [
-        pltpu.make_async_copy(s, d, in_sem.at[i])
-        for i, (s, d) in enumerate(
-            [(ids, ids_v), (lens, lens_v), (pin, pin_v), (pool, pool_v), (pout, pout_v)]
-        )
-    ]
-    for copy in loads:
-        copy.start()
-    chunks = [
-        pltpu.make_async_copy(grads.at[pl.ds(e * slots, slots)], grads_v.at[e], g_sem.at[e])
-        for e in range(examples)
-    ]
-    for copy in chunks:
-        copy.start()
-    own_q = pltpu.make_async_copy(qs, qall.at[x, z, c], q_local)
-    own_q.start()
-
     def device(px, pz, pc):
         return {"dp": (px * NZ + pz) * NC + pc}
 
@@ -75,6 +59,23 @@
     for friend in friends:
         pl.semaphore_signal(barrier, inc=1, device_id=friend, device_id_type=MESH)
 
+    loads = [
+        pltpu.make_async_copy(s, d, in_sem.at[i])
+        for i, (s, d) in enumerate(
+            [(ids, ids_v), (lens, lens_v), (pin, pin_v), (pool, pool_v), (pout, pout_v)]
+        )
+    ]
+    for copy in loads:
+        copy.start()
+    chunks = [
+        pltpu.make_async_copy(grads.at[pl.ds(e * slots, slots)], grads_v.at[e], g_sem.at[e])
+        for e in range(examples)
+    ]
+    for copy in chunks:
+        copy.start()
+    own_q = pltpu.make_async_copy(qs, qall.at[x, z, c], q_local)
+    own_q.start()
+
     def remote(src, dst, send, recv, to):
         return pltpu.make_async_remote_copy(
             src_ref=src, dst_ref=dst, send_sem=send, recv_sem=recv,
@@ -88,9 +89,8 @@
 
     sent = []
 
-    for copy in loads[:4]:
-        copy.wait()
-    p_send[...] = dot_nt(pin_v[...], pool_v[...]).reshape(p_send.shape)
+    loads[0].wait()
+    loads[1].wait()
     rows = lax.broadcasted_iota(jnp.int32, (pool_v.shape[0], 128), 0)
     lane = lax.broadcasted_iota(jnp.int32, (1, 128), 1)
     scale = lax.rsqrt(lens_v[...].astype(F32))
@@ -100,17 +100,15 @@
             row = (e * slots + first) // 128
             token = jnp.where(lane + first < length, ids_v[row:row + 1, :], -1)
             pick_v[e, :, first:first + 128] = jnp.where(rows == token, 1.0, 0.0).astype(BF16)
-    loads[4].wait()
 
     def project(e):
-        chunks[e].wait()
         high, low = split(dot_nt(pout_v[...], grads_v[e]))
         n = high.shape[0]
-        cat_v[e % 2, :n, :] = high
-        cat_v[e % 2, n:, :] = low
+        cat_v[e, :n, :] = high
+        cat_v[e, n:, :] = low
 
     def gather(e):
-        both = dot_nt(cat_v[e % 2], pick_v[e])
+        both = dot_nt(cat_v[e], pick_v[e])
         n = both.shape[0] // 2
         total = ((both[:n] + both[n:]) * scale[:, e:e + 1]).astype(BF16)
         share = n // T
@@ -118,37 +116,56 @@
             s_send[p, e, :share] = total[p * share:(p + 1) * share]
             s_send[p, e, share:] = total[n // 2 + p * share:n // 2 + (p + 1) * share]
 
-    project(0)
-    project(1)
-    gather(0)
-
-    pl.semaphore_wait(barrier, len(friends))
     p_out = [
         remote(p_send.at[p], p_recv.at[y], p_s.at[k], p_r.at[k], {"tensor": zh * NY + p})
         for k, p in enumerate(y_to)
     ]
-    start(p_out)
     q_z = [
         remote(qs, qall.at[x, z, c], qz_s.at[k], qz_r.at[k], device(x, p, c))
         for k, p in enumerate(z_to)
     ]
-    start(q_z)
-
-    def along_x(step, pz):
-        block = qall.at[x, pz, c]
+
+    def along_x(step, pz, block):
         return [
-            remote(block, block, qx_s.at[k, step], qx_r.at[k, step], device(p, z, c))
+            remote(block, qall.at[x, pz, c], qx_s.at[k, step], qx_r.at[k, step], device(p, z, c))
             for k, p in enumerate(x_to)
         ]
 
-    own_q.wait()
-    start(along_x(0, z))
-
+    q_x = along_x(0, z, qs)
+    sent.extend(p_out + q_z + q_x)
+
+    def gate():
+        pl.semaphore_wait(barrier, len(friends))
+        for copy in p_out + q_z + q_x:
+            copy.start()
+
+    def gate_at(place):
+        if GATES[0] == place and GATES[1] == place:
+            gate()
+        elif GATES[0] == place:
+            pl.when(zh == 0)(gate)
+        elif GATES[1] == place:
+            pl.when(zh != 0)(gate)
+
+    for copy in loads[2:]:
+        copy.wait()
+    p_send[...] = dot_nt(pin_v[...], pool_v[...]).reshape(p_send.shape)
+    gate_at(0)
+    chunks[0].wait()
+    project(0)
+    gate_at(1)
+    chunks[1].wait()
+    project(1)
+    gather(0)
+    gate_at(2)
+    chunks[2].wait()
+    chunks[3].wait()
     project(2)
     gather(1)
     project(3)
     gather(2)
     gather(3)
+    gate_at(3)
     s_out = [
         remote(s_send.at[p], s_recv.at[y], s_s.at[k], s_r.at[k], {"tensor": zh * NY + p})
         for k, p in enumerate(y_to)
@@ -167,12 +184,13 @@
 
     for k in range(NZ - 1):
         remote(qs, qall.at[x, z_from[k], c], qz_s.at[k], qz_r.at[k], other).wait_recv()
-        start(along_x(k + 1, z_from[k]))
+        start(along_x(k + 1, z_from[k], qall.at[x, z_from[k], c]))
 
     def across(k, px):
         line = qall.at[px, :, c]
         return remote(line, line, qc_s.at[k], qc_r.at[k], other)
 
+    own_q.wait()
     start([across(0, x)])
 
     s_recv[y] = s_send[y]
@@ -226,14 +244,6 @@
 
     for copy in sent:
         copy.wait_send()
-
-
-def finish(a, b, a_out, b_out, sems):
-    copies = [pltpu.make_async_copy(a, a_out, sems.at[0]), pltpu.make_async_copy(b, b_out, sems.at[1])]
-    for copy in copies:
-        copy.start()
-    for copy in copies:
-        copy.wait()
 
 
 def local(pool_rows, out_grads, proj_in, proj_out, token_ids, lengths, queries):
@@ -247,11 +257,11 @@
     any_spec = pl.BlockSpec(memory_space=pl.ANY)
     dma = pltpu.SemaphoreType.DMA
     vmem = pltpu.VMEM
-    sketches, scores = pl.pallas_call(
+    return pl.pallas_call(
         kernel,
         out_shape=(
-            jax.ShapeDtypeStruct((examples, share * width), F32),
-            jax.ShapeDtypeStruct((examples, rows * NX * NZ * NC), F32),
+            vmem((examples, share * width), F32),
+            vmem((examples, rows * NX * NZ * NC), F32),
         ),
         in_specs=[any_spec] * 7,
         out_specs=[pl.BlockSpec(memory_space=pltpu.VMEM)] * 2,
@@ -264,7 +274,7 @@
             vmem((1, examples), jnp.int32),
             vmem((NX, NZ, NC, rows, cols), BF16),
             vmem((examples, pool, slots), BF16),
-            vmem((2, 2 * width, slots), BF16),
+            vmem((examples, 2 * width, slots), BF16),
             vmem((NY, width // NY, pool), F32),
             vmem((NY, width // NY, pool), F32),
             vmem((T, width // NY, pool), F32),
@@ -287,17 +297,6 @@
         pool_rows, out_grads, proj_in.T, proj_out.T,
         token_ids.reshape(-1, 128), lengths.reshape(1, -1), queries,
     )
-    return pl.pallas_call(
-        finish,
-        out_shape=(
-            jax.ShapeDtypeStruct(sketches.shape, F32),
-            jax.ShapeDtypeStruct(scores.shape, F32),
-        ),
-        in_specs=[any_spec] * 2,
-        out_specs=[any_spec] * 2,
-        scratch_shapes=[dma((2,))],
-        compiler_params=pltpu.CompilerParams(vmem_limit_bytes=60 * 1024 * 1024),
-    )(sketches, scores)
 
 
 def solution(mesh):

time: 38.6 us -> 33.8 us (0.88)
  Pallas kernels: 37.8 us -> 31.9 us
  local copies, waits for them, and re-layouts: 0 us -> 1.21 us
    pallas_call x2 -> x1, Pallas kernels: 37.8 us -> 31.9 us  [local(): pl.pallas_call(kernel, out_shape=(vmem((examples, share * width), F32), v...]
    unnamed x0 -> x2, local copies, waits for them, and re-layouts: none -> 1.21 us
where the time goes in v3:
time: 33.8 us; the launch traced here: 33.7 us
  Pallas kernels  31.9 us (94%)
  local copies, waits for them, and re-layouts  1.21 us (4%)
  between operations  0.64 us (2%)
    pallas_call x1, Pallas kernels, local(): pl.pallas_call(kernel, out_shape=(vmem((examples, share * width), F32), v...  31.9 us
    unnamed x2, local copies, waits for them, and re-layouts  1.21 us

profile of v3, /device:TPU:1, one launch (start us, length us, event | category | flops | bytes accessed | tf_op | source)
XLA Modules:
  0.0 33.7 jit_solution(15821135002946198456)
XLA Ops:
  0.6 31.9 %shard_map.86 = (f32[4,512]{1,0:T(4,128)S(1)}, f32[4,1024]{1,0:T(4,128)S(1)}) custom-call(bf16[256,3584]{1,0:T(8,128)(2,1)} %pool.1, bf16[4096,1024]{1,0:T(8,128)(2,1)} %grads.1, bf16[64,3584]{1,0:T(8,128)(2,1)} %bitcast.4, bf16[64,1024]{1,0:T(8,128)(2,1)} %bitcast.5, s32[32,128]{1,0:T(8,128)} %bitcast.6, s32[1,4]{1,0:T(1,128)} %bitcast.7, bf16[32,512]{1,0:T(8,128)(2,1)} %qs.1), custom_call_target="tpu_custom_call" | custom-call | tf_op jit(solution)/shard_map/pallas_call | solution.py:260
  32.5 0.6 %copy.11 = f32[4,512]{1,0:T(4,128)} copy(f32[4,512]{1,0:T(4,128)S(1)} %get-tuple-element.2) | data formatting | bytes 16384
  33.1 0.6 %copy.12 = f32[4,1024]{1,0:T(4,128)} copy(f32[4,1024]{1,0:T(4,128)S(1)} %get-tuple-element.3) | data formatting | bytes 32768

commit v4 on v3

--- a/solution.py
+++ b/solution.py
@@ -10,6 +10,7 @@
 T = 8
 NY = 4
 GATES = 3, 0
+FAR = 2, 1, 3, 0, 2, 1, 3
 NX, NZ, NC = 4, 4, 2
 
 
@@ -41,20 +42,20 @@
         return {"dp": (px * NZ + pz) * NC + pc}
 
     def peer(k):
-        return lax.rem(me + k, T)
+        half = (1 - zh) if k < NY else zh
+        return half * NY + (y + FAR[k]) % NY
 
     y_to = [(y + k) % NY for k in range(1, NY)]
-    z_to = [(z + k) % NZ for k in range(1, NZ)]
-    z_from = [(z + NZ - k) % NZ for k in range(1, NZ)]
-    x_to = [(x + k) % NX for k in range(1, NX)]
-    x_from = [(x + NX - k) % NX for k in range(1, NX)]
+    z_near = [z + 1 - 2 * (z % 2), 2 - z // 2, 3 - 3 * (z // 2)]
+    x_to = [(x + k) % NX for k in (2, 1, 3)]
+    x_from = [(x + NX - k) % NX for k in (2, 1, 3)]
     other = device(x, z, 1 - c)
     partner = {"tensor": (1 - zh) * NY + y}
 
     barrier = pltpu.get_barrier_semaphore()
     friends = [partner, other]
     friends += [{"tensor": zh * NY + p} for p in y_to]
-    friends += [device(x, p, c) for p in z_to]
+    friends += [device(x, p, c) for p in z_near]
     friends += [device(p, z, c) for p in x_to]
     for friend in friends:
         pl.semaphore_signal(barrier, inc=1, device_id=friend, device_id_type=MESH)
@@ -121,18 +122,25 @@
         for k, p in enumerate(y_to)
     ]
     q_z = [
-        remote(qs, qall.at[x, z, c], qz_s.at[k], qz_r.at[k], device(x, p, c))
-        for k, p in enumerate(z_to)
-    ]
-
-    def along_x(step, pz, block):
+        remote(qs, qall.at[x, z, c], qz_s.at[k], qz_r.at[z], device(x, z_near[k], c))
+        for k in (2, 1, 0)
+    ]
+
+    def along_x(pz, block):
         return [
-            remote(block, qall.at[x, pz, c], qx_s.at[k, step], qx_r.at[k, step], device(p, z, c))
+            remote(block, qall.at[x, pz, c], qx_s.at[k, pz], qx_r.at[k, pz], device(p, z, c))
             for k, p in enumerate(x_to)
         ]
 
-    q_x = along_x(0, z, qs)
-    sent.extend(p_out + q_z + q_x)
+    q_x = along_x(z, qs)
+    q_on = [along_x(z_near[k], qall.at[x, z_near[k], c]) for k in range(NZ - 1)]
+    sent.extend(p_out + q_z + q_x + sum(q_on, []))
+
+    def pass_on(k):
+        block = qall.at[x, z_near[k], c]
+        remote(block, block, qz_s.at[k], qz_r.at[z_near[k]], other).wait_recv()
+        for copy in q_on[k]:
+            copy.start()
 
     def gate():
         pl.semaphore_wait(barrier, len(friends))
@@ -162,6 +170,7 @@
     chunks[3].wait()
     project(2)
     gather(1)
+    pl.when(zh != 0)(lambda: pass_on(0))
     project(3)
     gather(2)
     gather(3)
@@ -172,26 +181,35 @@
     ]
     start(s_out)
 
+    pl.when(zh == 0)(lambda: pass_on(0))
+
     p_recv[y] = p_send[y]
     for copy in p_out:
         copy.wait_recv()
     p_part[me] = jnp.sum(p_recv[...], axis=0)
     a_out = [
-        remote(p_part.at[me], p_part.at[me], a_s.at[k - 1], a_r.at[k - 1], {"tensor": peer(k)})
-        for k in range(1, T)
+        remote(p_part.at[me], p_part.at[me], a_s.at[k], a_r.at[k], {"tensor": peer(k)})
+        for k in range(T - 1)
     ]
     start(a_out)
 
-    for k in range(NZ - 1):
-        remote(qs, qall.at[x, z_from[k], c], qz_s.at[k], qz_r.at[k], other).wait_recv()
-        start(along_x(k + 1, z_from[k], qall.at[x, z_from[k], c]))
-
-    def across(k, px):
-        line = qall.at[px, :, c]
-        return remote(line, line, qc_s.at[k], qc_r.at[k], other)
+    pass_on(1)
+    pass_on(2)
+
+    def across(px, pz):
+        block = qall.at[px, pz, c]
+        copy = remote(block, block, qc_s.at[px, pz], qc_r.at[px, pz], other)
+        copy.start()
+        return copy
+
+    def arrived(k, pz):
+        block = qall.at[x_from[k], pz, c]
+        remote(block, block, qx_s.at[k, pz], qx_r.at[k, pz], other).wait_recv()
+        return across(x_from[k], pz)
 
     own_q.wait()
-    start([across(0, x)])
+    sent += [across(x, z)] + [across(x, pz) for pz in z_near]
+    sent += [arrived(k, z) for k in (1, 2, 0)]
 
     s_recv[y] = s_send[y]
     for copy in s_out:
@@ -203,38 +221,33 @@
     z_out = remote(z_send.at[:, 1 - zh], z_recv, z_s, z_r, partner)
     start([z_out])
 
-    for k in range(NX - 1):
-        for step in range(NZ):
-            pz = z if step == 0 else z_from[step - 1]
-            block = qall.at[x_from[k], pz, c]
-            remote(block, block, qx_s.at[k, step], qx_r.at[k, step], other).wait_recv()
-        start([across(k + 1, x_from[k])])
+    for pz in z_near:
+        sent += [arrived(k, pz) for k in (1, 2, 0)]
 
     for copy in a_out:
         copy.wait_recv()
     p_all = p_part[0:NY] + p_part[NY:T]
     p_high, p_low = split(p_all.reshape(NY * p_all.shape[1], p_all.shape[2]))
+    p_cat = jnp.concatenate([p_high, p_high, p_low], 1)
 
     z_out.wait_recv()
     mine = z_send[:, zh] + z_recv[...]
     share = mine.shape[1]
     t_high, t_low = split(mine.reshape(examples * share, mine.shape[2]))
-    n = t_high.shape[0]
-    both = dot_nt(jnp.concatenate([t_high, t_low], 0), p_high)
-    sk_v[...] = both[:n] + both[n:] + dot_nt(t_high, p_low)
+    sk_v[...] = dot_nt(jnp.concatenate([t_high, t_low, t_high], 1), p_cat)
     flat = jnp.concatenate([sk_v[pl.ds(a, examples, stride=share), :] for a in range(share)], 1)
     sk_out[...] = flat
 
-    for k in range(NX):
-        px = x if k == 0 else x_from[k - 1]
-        line = qall.at[px, :, 1 - c]
-        remote(line, line, qc_s.at[k], qc_r.at[k], other).wait_recv()
+    for pz in [z] + z_near:
+        for px in [x] + x_from:
+            block = qall.at[px, pz, 1 - c]
+            remote(block, block, qc_s.at[px, pz], qc_r.at[px, pz], other).wait_recv()
     queries = qall[...].reshape(-1, flat.shape[1])
     part = dot_nt(jnp.concatenate(split(flat), 0), queries)
     c_send[...] = part[:examples] + part[examples:]
     c_out = [
-        remote(c_send, c_recv.at[me], c_s.at[k - 1], c_r.at[k - 1], {"tensor": peer(k)})
-        for k in range(1, T)
+        remote(c_send, c_recv.at[me], c_s.at[k], c_r.at[k], {"tensor": peer(k)})
+        for k in range(T - 1)
     ]
     start(c_out)
     c_recv[me] = c_send[...]
@@ -286,7 +299,7 @@
             vmem((examples, rows * NX * NZ * NC), F32),
             vmem((T, examples, rows * NX * NZ * NC), F32),
             dma((5,)), dma((examples,)), dma(()),
-            dma((3,)), dma((3,)), dma((3, NZ)), dma((3, NZ)), dma((NX,)), dma((NX,)),
+            dma((3,)), dma((NZ,)), dma((3, NZ)), dma((3, NZ)), dma((NX, NZ)), dma((NX, NZ)),
             dma((3,)), dma((3,)), dma((T - 1,)), dma((T - 1,)),
             dma((3,)), dma((3,)), dma(()), dma(()), dma((T - 1,)), dma((T - 1,)),
         ],

time: 33.8 us -> 33 us (0.976)
  Pallas kernels: 31.9 us -> 31 us
    pallas_call x1, Pallas kernels: 31.9 us -> 31 us  [local(): pl.pallas_call(kernel, out_shape=(vmem((examples, share * width), F32), v...]
where the time goes in v4:
time: 33 us; the launch traced here: 32.9 us
  Pallas kernels  31 us (94%)
  local copies, waits for them, and re-layouts  1.21 us (4%)
  between operations  0.64 us (2%)
    pallas_call x1, Pallas kernels, local(): pl.pallas_call(kernel, out_shape=(vmem((examples, share * width), F32), v...  31 us
    unnamed x2, local copies, waits for them, and re-layouts  1.21 us

profile of v4, /device:TPU:1, one launch (start us, length us, event | category | flops | bytes accessed | tf_op | source)
XLA Modules:
  0.0 32.9 jit_solution(16034692979319075041)
XLA Ops:
  0.6 31.0 %shard_map.86 = (f32[4,512]{1,0:T(4,128)S(1)}, f32[4,1024]{1,0:T(4,128)S(1)}) custom-call(bf16[256,3584]{1,0:T(8,128)(2,1)} %pool.1, bf16[4096,1024]{1,0:T(8,128)(2,1)} %grads.1, bf16[64,3584]{1,0:T(8,128)(2,1)} %bitcast.4, bf16[64,1024]{1,0:T(8,128)(2,1)} %bitcast.5, s32[32,128]{1,0:T(8,128)} %bitcast.6, s32[1,4]{1,0:T(1,128)} %bitcast.7, bf16[32,512]{1,0:T(8,128)(2,1)} %qs.1), custom_call_target="tpu_custom_call" | custom-call | tf_op jit(solution)/shard_map/pallas_call | solution.py:273
  31.7 0.6 %copy.11 = f32[4,512]{1,0:T(4,128)} copy(f32[4,512]{1,0:T(4,128)S(1)} %get-tuple-element.2) | data formatting | bytes 16384
  32.3 0.6 %copy.12 = f32[4,1024]{1,0:T(4,128)} copy(f32[4,1024]{1,0:T(4,128)S(1)} %get-tuple-element.3) | data formatting | bytes 32768

commit v5 on v4

--- a/solution.py
+++ b/solution.py
@@ -111,11 +111,12 @@
     def gather(e):
         both = dot_nt(cat_v[e], pick_v[e])
         n = both.shape[0] // 2
-        total = ((both[:n] + both[n:]) * scale[:, e:e + 1]).astype(BF16)
+        total = (both[:n] + both[n:]) * scale[:, e:e + 1]
         share = n // T
         for p in range(NY):
-            s_send[p, e, :share] = total[p * share:(p + 1) * share]
-            s_send[p, e, share:] = total[n // 2 + p * share:n // 2 + (p + 1) * share]
+            low, high = p * share, n // 2 + p * share
+            pair = jnp.concatenate([total[low:low + share], total[high:high + share]], 0)
+            s_send[p, e] = pair.astype(BF16)
 
     p_out = [
         remote(p_send.at[p], p_recv.at[y], p_s.at[k], p_r.at[k], {"tensor": zh * NY + p})

time: 33 us -> 33 us (level)
  no operation moved by 1% of the time
where the time goes in v5:
time: 33 us; the launch traced here: 32.9 us
  Pallas kernels  31 us (94%)
  local copies, waits for them, and re-layouts  1.21 us (4%)
  between operations  0.64 us (2%)
    pallas_call x1, Pallas kernels, local(): pl.pallas_call(kernel, out_shape=(vmem((examples, share * width), F32), v...  31 us
    unnamed x2, local copies, waits for them, and re-layouts  1.21 us

profile of v5, /device:TPU:1, one launch (start us, length us, event | category | flops | bytes accessed | tf_op | source)
XLA Modules:
  0.0 32.9 jit_solution(16034692979319075041)
XLA Ops:
  0.6 31.0 %shard_map.86 = (f32[4,512]{1,0:T(4,128)S(1)}, f32[4,1024]{1,0:T(4,128)S(1)}) custom-call(bf16[256,3584]{1,0:T(8,128)(2,1)} %pool.1, bf16[4096,1024]{1,0:T(8,128)(2,1)} %grads.1, bf16[64,3584]{1,0:T(8,128)(2,1)} %bitcast.4, bf16[64,1024]{1,0:T(8,128)(2,1)} %bitcast.5, s32[32,128]{1,0:T(8,128)} %bitcast.6, s32[1,4]{1,0:T(1,128)} %bitcast.7, bf16[32,512]{1,0:T(8,128)(2,1)} %qs.1), custom_call_target="tpu_custom_call" | custom-call | tf_op jit(solution)/shard_map/pallas_call | solution.py:274
  31.7 0.6 %copy.11 = f32[4,512]{1,0:T(4,128)} copy(f32[4,512]{1,0:T(4,128)S(1)} %get-tuple-element.2) | data formatting | bytes 16384
  32.3 0.6 %copy.12 = f32[4,1024]{1,0:T(4,128)} copy(f32[4,1024]{1,0:T(4,128)S(1)} %get-tuple-element.3) | data formatting | bytes 32768

commit v6 on v5

--- a/solution.py
+++ b/solution.py
@@ -53,10 +53,10 @@
     partner = {"tensor": (1 - zh) * NY + y}
 
     barrier = pltpu.get_barrier_semaphore()
-    friends = [partner, other]
-    friends += [{"tensor": zh * NY + p} for p in y_to]
-    friends += [device(x, p, c) for p in z_near]
+    friends = [partner]
     friends += [device(p, z, c) for p in x_to]
+    friends += [{"tensor": zh * NY + (y + k) % NY} for k in (2, 1, 3)]
+    friends += [device(x, p, c) for p in z_near[::-1]] + [other]
     for friend in friends:
         pl.semaphore_signal(barrier, inc=1, device_id=friend, device_id_type=MESH)
 
@@ -116,7 +116,7 @@
         for p in range(NY):
             low, high = p * share, n // 2 + p * share
             pair = jnp.concatenate([total[low:low + share], total[high:high + share]], 0)
-            s_send[p, e] = pair.astype(BF16)
+            s_send[p, e] = pair
 
     p_out = [
         remote(p_send.at[p], p_recv.at[y], p_s.at[k], p_r.at[k], {"tensor": zh * NY + p})
@@ -215,9 +215,7 @@
     s_recv[y] = s_send[y]
     for copy in s_out:
         copy.wait_recv()
-    over_y = s_recv[0].astype(F32)
-    for p in range(1, NY):
-        over_y = over_y + s_recv[p].astype(F32)
+    over_y = jnp.sum(s_recv[...], axis=0)
     z_send[...] = over_y.reshape(z_send.shape)
     z_out = remote(z_send.at[:, 1 - zh], z_recv, z_s, z_r, partner)
     start([z_out])
@@ -292,8 +290,8 @@
             vmem((NY, width // NY, pool), F32),
             vmem((NY, width // NY, pool), F32),
             vmem((T, width // NY, pool), F32),
-            vmem((NY, examples, 2 * share, pool), BF16),
-            vmem((NY, examples, 2 * share, pool), BF16),
+            vmem((NY, examples, 2 * share, pool), F32),
+            vmem((NY, examples, 2 * share, pool), F32),
             vmem((examples, 2, share, pool), F32),
             vmem((examples, share, pool), F32),
             vmem((examples * share, width), F32),

time: 33 us -> 33 us (level)
  no operation moved by 1% of the time
where the time goes in v6:
time: 33 us; the launch traced here: 32.9 us
  Pallas kernels  31 us (94%)
  local copies, waits for them, and re-layouts  1.21 us (4%)
  between operations  0.64 us (2%)
    pallas_call x1, Pallas kernels, local(): pl.pallas_call(kernel, out_shape=(vmem((examples, share * width), F32), v...  31 us
    unnamed x2, local copies, waits for them, and re-layouts  1.21 us

profile of v6, /device:TPU:1, one launch (start us, length us, event | category | flops | bytes accessed | tf_op | source)
XLA Modules:
  0.0 32.9 jit_solution(17649588261536417549)
XLA Ops:
  0.6 31.0 %shard_map.86 = (f32[4,512]{1,0:T(4,128)S(1)}, f32[4,1024]{1,0:T(4,128)S(1)}) custom-call(bf16[256,3584]{1,0:T(8,128)(2,1)} %pool.1, bf16[4096,1024]{1,0:T(8,128)(2,1)} %grads.1, bf16[64,3584]{1,0:T(8,128)(2,1)} %bitcast.4, bf16[64,1024]{1,0:T(8,128)(2,1)} %bitcast.5, s32[32,128]{1,0:T(8,128)} %bitcast.6, s32[1,4]{1,0:T(1,128)} %bitcast.7, bf16[32,512]{1,0:T(8,128)(2,1)} %qs.1), custom_call_target="tpu_custom_call" | custom-call | tf_op jit(solution)/shard_map/pallas_call | solution.py:272
  31.7 0.6 %copy.11 = f32[4,512]{1,0:T(4,128)} copy(f32[4,512]{1,0:T(4,128)S(1)} %get-tuple-element.2) | data formatting | bytes 16384
  32.3 0.6 %copy.12 = f32[4,1024]{1,0:T(4,128)} copy(f32[4,1024]{1,0:T(4,128)S(1)} %get-tuple-element.3) | data formatting | bytes 32768
